TPU v7x, 32 devices: a whole 2x2x4 slice. The times are simulated.
32 devices in a mesh: tower: 2 (over core), section: 4 (over y, x), tp: 4 (over z).
Axes of the slice: x: 2, y: 2, z: 4, core: 2. Of those that a mesh axis runs over, the one named last changes fastest.
Arguments:
- in_flight: bfloat16 [2, 4, 430080], P('tower', 'section', 'tp'), may hold values from -6 to 6
- fresh: bfloat16 [2, 3, 430080], P('tower', None, 'tp'), may hold values from -6 to 6
- wide_proj: bfloat16 [2, 4, 2, 5120, 2048], P('tower', 'section', None, None, 'tp'), may hold values from -0.024317239 to 0.024317239
- narrow_proj: bfloat16 [2, 4, 2, 1792, 2048], P('tower', 'section', None, None, 'tp'), may hold values from -0.041103636 to 0.041103636
- gain_vis: bfloat16 [4, 1792], P('section'), may hold values from 0.25 to 1.75
- gain_txt: bfloat16 [4, 5120], P('section'), may hold values from 0.25 to 1.75
- text_len: int32 [7], replicated, may hold values from 21 to 84, as said below
- vis_len: int32 [7], replicated, may hold values from 60 to 240, as said below
Outputs:
- section_out: bfloat16 [2, 4, 4, 430080], P('tower', 'section', None, 'tp')
Inputs may be any that keep to these rules, and one draw needn't show every extreme that they name: `text_len`: some micro-batch has all 84 tokens live. `vis_len`: some micro-batch has all 240 patches live.
All inputs are finite; a program needn't handle non-finite values.
Results may differ from a plain program's by a relative error of at most 0.02.
Values may be sent and summed in bfloat16 or wider, within the bound.
A program may use at most 128 MiB of HBM per device.

v0:
```python
import jax
import jax.numpy as jnp
from jax import lax
from jax.sharding import PartitionSpec as P

HDIM = 64


def swapped(x, axis, apart):
    return lax.ppermute(x, axis, [(i, i ^ 1 << apart) for i in range(lax.axis_size(axis))])


def shifted(value, axis, steps):
    count = lax.axis_size(axis)
    initial, last = (max(0, -steps), min(count, count - steps))
    return lax.ppermute(value, axis, [(source, source + steps) for source in range(initial, last)])


def normed(stream, gain):
    values = stream.astype(jnp.float32)
    scale = lax.rsqrt(jnp.mean(values * values, axis=-1, keepdims=True) + 1e-06)
    return (values * scale * gain.astype(jnp.float32)).astype(jnp.bfloat16)


def unpack(packed, groups, rows, width):
    return packed.reshape(groups, rows, width // groups).transpose(1, 0, 2).reshape(rows, width)


def pack_term(term, groups):
    rows, width = term.shape
    return term.reshape(rows, groups, width // groups).transpose(1, 0, 2).reshape(groups, -1)


def attend(query_src, key_src, query_w, key_w, value_w, live):
    rows_q = query_src.shape[0]
    rows_k = key_src.shape[0]
    heads_here = query_w.shape[1] // HDIM
    query = jnp.dot(query_src, query_w, preferred_element_type=jnp.float32).astype(jnp.bfloat16)
    keys = jnp.dot(key_src, key_w, preferred_element_type=jnp.float32).astype(jnp.bfloat16)
    values = jnp.dot(key_src, value_w, preferred_element_type=jnp.float32).astype(jnp.bfloat16)
    query = query.reshape(rows_q, heads_here, HDIM)
    keys = keys.reshape(rows_k, heads_here, HDIM)
    values = values.reshape(rows_k, heads_here, HDIM)
    scores = jnp.einsum("qhd,khd->hqk", query, keys, preferred_element_type=jnp.float32)
    scores = scores / jnp.sqrt(jnp.float32(HDIM))
    alive = jnp.arange(rows_k, dtype=jnp.int32) < live
    scores = jnp.where(alive[None, None, :], scores, jnp.float32(-1e30))
    weights = jnp.exp(scores)
    probs = (weights / jnp.sum(weights, axis=-1, keepdims=True)).astype(jnp.bfloat16)
    attended = jnp.einsum("hqk,khd->qhd", probs, values, preferred_element_type=jnp.float32)
    return attended.astype(jnp.bfloat16).reshape(rows_q, heads_here * HDIM)


def project_out(attended, out_w):
    return jnp.einsum("rj,wj->rw", attended, out_w, preferred_element_type=jnp.float32)


def on_device(in_flight, fresh, wide_proj, narrow_proj, gain_vis, gain_txt, text_len, vis_len):
    sections = lax.axis_size("section")
    groups = lax.axis_size("tp")
    section_id = lax.axis_index("section")
    tower_id = lax.axis_index("tower")
    flat = in_flight.shape[2]
    ticks = fresh.shape[1] + 1
    vis_width = gain_vis.shape[1]
    txt_width = gain_txt.shape[1]
    vis_rows = flat * groups // vis_width
    txt_rows = flat * groups // txt_width
    wide = wide_proj[0, 0]
    narrow = narrow_proj[0, 0]
    first_vis = tower_id == 0
    own_block = in_flight[0, 0]
    records = []
    for tick in range(ticks):
        if tick > 0:
            passed = shifted(records[-1], "section", 1)
            own_block = jnp.where(section_id == 0, fresh[0, tick - 1], passed)
        flight = tick - section_id + sections - 1
        partner = swapped(own_block, "tower", 0)
        own_all = lax.all_gather(own_block, "tp", axis=0, tiled=True)
        partner_all = lax.all_gather(partner, "tp", axis=0, tiled=True)
        vis_flat = jnp.where(first_vis, own_all, partner_all)
        txt_flat = jnp.where(first_vis, partner_all, own_all)
        vision = unpack(vis_flat, groups, vis_rows, vis_width)
        text = unpack(txt_flat, groups, txt_rows, txt_width)
        norm_vis = normed(vision, gain_vis[0])
        norm_txt = normed(text, gain_txt[0])
        live_txt = lax.dynamic_index_in_dim(text_len, flight, 0, keepdims=False)
        live_vis = lax.dynamic_index_in_dim(vis_len, flight, 0, keepdims=False)

        def vision_side():
            attended = attend(norm_vis, norm_txt, narrow[0], wide[0], wide[1], live_txt)
            return pack_term(project_out(attended, narrow[1]), groups)

        def text_side():
            attended = attend(norm_txt, norm_vis, wide[0], narrow[0], narrow[1], live_vis)
            return pack_term(project_out(attended, wide[1]), groups)

        term = lax.cond(first_vis, vision_side, text_side)
        summed = lax.psum_scatter(
            term.astype(jnp.bfloat16), "tp", scatter_dimension=0, tiled=True
        ).astype(jnp.float32)
        own_block = (own_block.astype(jnp.float32) + summed[0]).astype(jnp.bfloat16)
        records.append(own_block)
    return jnp.stack(records).reshape(1, 1, ticks, flat)


def solution(mesh):
    placed = (
        P("tower", "section", "tp"),
        P("tower", None, "tp"),
        P("tower", "section", None, None, "tp"),
        P("tower", "section", None, None, "tp"),
        P("section", None),
        P("section", None),
        P(),
        P(),
    )
    return jax.shard_map(
        on_device,
        mesh=mesh,
        in_specs=placed,
        out_specs=P("tower", "section", None, "tp"),
        check_vma=False,
    )
```

profile of v0, /device:TPU:12, one launch (start us, length us, event | category | flops | bytes accessed | tf_op | source)
XLA Modules:
  0.0 557.4 jit_solution(13941207614308702385)
XLA Ops:
  6.5 2.2 reduce.17
  8.8 32.9 %all-gather = bf16[1,1,430080]{2,1,0:T(2,128)(2,1)S(1)} all-gather(bf16[1,1,107520]{2,1,0:T(2,128)(2,1)} %param.16), channel_id=2, replica_groups=mesh['tower'=2,'section'=4,'tp'=4] {'tp'}, dimensions={2}, use_global_device_ids=true | all-gather | bytes 1075200 | tf_op jit(solution)/shard_map/all_gather | solution.py:80
  41.7 18.7 %reduce.16 = bf16[430080]{0:T(1024)(128)(2,1)} reduce(bf16[1,1,430080]{2,1,0:T(2,128)(2,1)S(1)} %all-gather, bf16[]{:T(256)} %constant.153), dimensions={0,1}, to_apply=%all-gather.reduce_sub_computation | reduce | bytes 1720322 | tf_op jit(solution)/shard_map/all_gather | solution.py:80
  60.5 19.0 %all_gather.25 = bf16[430080]{0:T(1024)(128)(2,1)S(1)} all-gather(bf16[107520]{0:T(1024)(128)(2,1)S(1)} %collective-permute-done), channel_id=1, replica_groups=mesh['tower'=2,'section'=4,'tp'=4] {'tp'}, dimensions={0}, use_global_device_ids=true | all-gather | bytes 1075200 | tf_op jit(solution)/shard_map/all_gather | solution.py:81
  79.5 4.2 fusion.191
  88.4 1.9 reshape.342
  90.3 1.8 copy.177
  92.1 1.9 mul.191
  94.2 1.8 multiply_convert_fusion.3
  96.9 15.4 %conditional.4 = (bf16[4,107520]{1,0:T(4,128)(2,1)S(1)}) conditional(s32[]{:T(128)} %convert_element_type.379, (bf16[2,1792,512]{2,1,0:T(8,128)(2,1)}, bf16[240,1792]{0,1:T(8,128)(2,1)S(1)}, s32[7]{0:T(128)S(1)}, s32[]{:T(128)}, bf16[2,5120,512]{2,1,0:T(8,128)(2,1)}, /*index=5*/bf16[84,5120]{1,0:T(8,128)(2,1)S(1)}) %tuple.104, ...), branch_computations={%region_2.4_spmd, %region_4.6_spmd} | conditional | flops 1803874432 | bytes 33575416 | solution.py:99
  97.0 3.4 fusion.39
  100.6 2.1 fusion.33
  104.5 3.4 fusion.36
  113.9 46.8 %all-reduce.9.cloned.1.call-done = bf16[4,107520]{1,0:T(4,128)(2,1)} async-done(((bf16[4,107520]{1,0:T(4,128)(2,1)}), bf16[4,107520]{1,0:T(4,128)(2,1)}) %all-reduce.9.cloned.1.call-update) | async-done | bytes 860176
  160.7 3.3 fusion.184
  164.1 3.6 collective-permute-start.1
  167.7 4.3 slice_reduce_fusion.2
  172.0 1.7 collective-permute-done.1
  173.8 17.6 %all_gather.26 = bf16[430080]{0:T(1024)(128)(2,1)S(1)} all-gather(bf16[107520]{0:T(1024)(128)(2,1)S(1)} %broadcast_select_fusion.2), channel_id=1, replica_groups=mesh['tower'=2,'section'=4,'tp'=4] {'tp'}, dimensions={0}, use_global_device_ids=true | all-gather | bytes 1075200 | tf_op jit(solution)/shard_map/all_gather | solution.py:80
  191.4 18.8 %all_gather.27 = bf16[430080]{0:T(1024)(128)(2,1)S(1)} all-gather(bf16[107520]{0:T(1024)(128)(2,1)S(1)} %collective-permute-done.2), channel_id=1, replica_groups=mesh['tower'=2,'section'=4,'tp'=4] {'tp'}, dimensions={0}, use_global_device_ids=true | all-gather | bytes 1075200 | tf_op jit(solution)/shard_map/all_gather | solution.py:81
  210.3 3.0 fusion.189
  218.0 1.9 reshape.344
  219.9 1.8 copy.181
  221.7 1.9 mul.207
  223.7 1.8 multiply_convert_fusion.2
  226.4 15.6 %conditional.5 = (bf16[4,107520]{1,0:T(4,128)(2,1)S(1)}) conditional(s32[]{:T(128)} %convert_element_type.379, (bf16[2,1792,512]{2,1,0:T(8,128)(2,1)}, bf16[240,1792]{0,1:T(8,128)(2,1)S(1)}, s32[7]{0:T(128)S(1)}, s32[]{:T(128)}, bf16[2,5120,512]{2,1,0:T(8,128)(2,1)}, /*index=5*/bf16[84,5120]{1,0:T(8,128)(2,1)S(1)}) %tuple.105, ...), branch_computations={%region_9.11_spmd, %region_11.13_spmd} | conditional | flops 1803874432 | bytes 33575416 | solution.py:99
  226.8 3.4 fusion.83
  230.4 2.1 fusion.77
  234.2 3.4 fusion.80
  243.0 46.5 %all-reduce.11.cloned.1.call-done = bf16[4,107520]{1,0:T(4,128)(2,1)} async-done(((bf16[4,107520]{1,0:T(4,128)(2,1)}), bf16[4,107520]{1,0:T(4,128)(2,1)}) %all-reduce.11.cloned.1.call-update) | async-done | bytes 860176
  289.5 2.2 dynamic-slice_convert_fusion.2
  291.8 3.4 collective-permute-start.3
  295.2 6.2 %collective-permute-done.3 = bf16[107520]{0:T(1024)(128)(2,1)S(1)} collective-permute-done((bf16[107520]{0:T(1024)(128)(2,1)S(1)}, bf16[107520]{0:T(1024)(128)(2,1)S(1)}, u32[]{:S(2)}, u32[]{:S(2)}) %collective-permute-start.3) | collective-permute-done | bytes 215072 | tf_op jit(solution)/shard_map/ppermute | solution.py:16
  301.5 17.6 %all_gather.28 = bf16[430080]{0:T(1024)(128)(2,1)S(1)} all-gather(bf16[107520]{0:T(1024)(128)(2,1)S(1)} %broadcast_select_fusion.1), channel_id=1, replica_groups=mesh['tower'=2,'section'=4,'tp'=4] {'tp'}, dimensions={0}, use_global_device_ids=true | all-gather | bytes 1075200 | tf_op jit(solution)/shard_map/all_gather | solution.py:80
  319.1 19.0 %all_gather.29 = bf16[430080]{0:T(1024)(128)(2,1)S(1)} all-gather(bf16[107520]{0:T(1024)(128)(2,1)S(1)} %collective-permute-done.4), channel_id=1, replica_groups=mesh['tower'=2,'section'=4,'tp'=4] {'tp'}, dimensions={0}, use_global_device_ids=true | all-gather | bytes 1075200 | tf_op jit(solution)/shard_map/all_gather | solution.py:81
  338.1 3.0 fusion.187
  341.2 1.7 reshape.347
  345.9 1.9 reshape.346
  347.8 1.8 copy.185
  349.5 1.9 mul.217
  351.6 1.8 multiply_convert_fusion.1
  354.3 15.5 %conditional.6 = (bf16[4,107520]{1,0:T(4,128)(2,1)S(1)}) conditional(s32[]{:T(128)} %convert_element_type.379, (bf16[2,1792,512]{2,1,0:T(8,128)(2,1)}, bf16[240,1792]{0,1:T(8,128)(2,1)S(1)}, s32[7]{0:T(128)S(1)}, s32[]{:T(128)}, bf16[2,5120,512]{2,1,0:T(8,128)(2,1)}, /*index=5*/bf16[84,5120]{1,0:T(8,128)(2,1)S(1)}) %tuple.106, ...), branch_computations={%region_16.18_spmd, %region_18.20_spmd} | conditional | flops 1803874432 | bytes 33575416 | solution.py:99
  354.5 3.4 fusion.127
  358.1 2.1 fusion.121
  362.0 3.4 fusion.124
  370.8 46.5 %all-reduce.13.cloned.1.call-done = bf16[4,107520]{1,0:T(4,128)(2,1)} async-done(((bf16[4,107520]{1,0:T(4,128)(2,1)}), bf16[4,107520]{1,0:T(4,128)(2,1)}) %all-reduce.13.cloned.1.call-update) | async-done | bytes 860176
  417.3 2.2 dynamic-slice_convert_fusion.1
  419.6 3.4 collective-permute-start.5
  423.0 6.2 %collective-permute-done.5 = bf16[107520]{0:T(1024)(128)(2,1)S(1)} collective-permute-done((bf16[107520]{0:T(1024)(128)(2,1)S(1)}, bf16[107520]{0:T(1024)(128)(2,1)S(1)}, u32[]{:S(2)}, u32[]{:S(2)}) %collective-permute-start.5) | collective-permute-done | bytes 215072 | tf_op jit(solution)/shard_map/ppermute | solution.py:16
  429.3 17.6 %all_gather.30 = bf16[430080]{0:T(1024)(128)(2,1)S(1)} all-gather(bf16[107520]{0:T(1024)(128)(2,1)S(1)} %broadcast_select_fusion), channel_id=1, replica_groups=mesh['tower'=2,'section'=4,'tp'=4] {'tp'}, dimensions={0}, use_global_device_ids=true | all-gather | bytes 1075200 | tf_op jit(solution)/shard_map/all_gather | solution.py:80
  446.9 18.8 %all_gather.31 = bf16[430080]{0:T(1024)(128)(2,1)S(1)} all-gather(bf16[107520]{0:T(1024)(128)(2,1)S(1)} %collective-permute-done.6), channel_id=1, replica_groups=mesh['tower'=2,'section'=4,'tp'=4] {'tp'}, dimensions={0}, use_global_device_ids=true | all-gather | bytes 1075200 | tf_op jit(solution)/shard_map/all_gather | solution.py:81
  465.8 3.0 fusion.185
  468.8 1.7 reshape.349
  473.5 1.9 reshape.348
  475.4 1.8 copy.189
  477.2 1.9 mul.227
  479.2 1.8 multiply_convert_fusion
  481.9 15.5 %conditional.7 = (bf16[4,107520]{1,0:T(4,128)(2,1)S(1)}) conditional(s32[]{:T(128)} %convert_element_type.379, (bf16[2,1792,512]{2,1,0:T(8,128)(2,1)}, bf16[240,1792]{0,1:T(8,128)(2,1)S(1)}, s32[7]{0:T(128)S(1)}, s32[]{:T(128)}, bf16[2,5120,512]{2,1,0:T(8,128)(2,1)}, /*index=5*/bf16[84,5120]{1,0:T(8,128)(2,1)S(1)}) %tuple.107, ...), branch_computations={%region_23.25_spmd, %region_25.27_spmd} | conditional | flops 1803874432 | bytes 33575416 | solution.py:99
  482.2 3.4 fusion.171
  485.7 2.1 fusion.165
  489.7 3.4 fusion.168
  498.9 46.1 %all-reduce.15.cloned.1.call-done = bf16[4,107520]{1,0:T(4,128)(2,1)} async-done(((bf16[4,107520]{1,0:T(4,128)(2,1)}), bf16[4,107520]{1,0:T(4,128)(2,1)}) %all-reduce.15.cloned.1.call-update) | async-done | bytes 860176
  545.0 2.2 dynamic-slice_convert_fusion
  547.5 2.9 maximum_bitcast_fusion
  (177 shorter events, 49.9 us)
Async XLA Ops:
  6.5 154.2 %all-reduce.9.cloned.1.call-start = ((), (), s32[]{:S(2)}) async-start(), calls=%async_computation | async-start | bytes 1720320
  8.7 51.7 %copy-start.23 = (bf16[107520]{0:T(1024)(128)(2,1)}, bf16[107520]{0:T(1024)(128)(2,1)S(1)}, u32[]{:S(2)}) copy-start(bf16[107520]{0:T(1024)(128)(2,1)S(1)} %reduce.17) | copy-start | bytes 645124
  8.7 51.8 %collective-permute-start = (bf16[107520]{0:T(1024)(128)(2,1)S(1)}, bf16[107520]{0:T(1024)(128)(2,1)S(1)}, u32[]{:S(2)}, u32[]{:S(2)}) collective-permute-start(bf16[107520]{0:T(1024)(128)(2,1)S(1)} %reduce.17), channel_id=1, source_target_pairs={{0,16},{16,0},{1,17},{17,1},{2,18},{18,2},{3,19},{19,3},{4,20},{20... | collective-permute-start | bytes 645128 | tf_op jit(solution)/shard_map/ppermute | solution.py:10
  41.7 18.7 %copy-start.25 = (bf16[1,5120]{1,0:T(2,128)(2,1)S(1)}, bf16[1,5120]{1,0:T(2,128)(2,1)}, u32[]{:S(2)}) copy-start(bf16[1,5120]{1,0:T(2,128)(2,1)} %param.21) | copy-start | bytes 30724
  41.7 18.8 %copy-start.26 = (bf16[1,1792]{1,0:T(2,128)(2,1)S(1)}, bf16[1,1792]{1,0:T(2,128)(2,1)}, u32[]{:S(2)}) copy-start(bf16[1,1792]{1,0:T(2,128)(2,1)} %param.20) | copy-start | bytes 10756
  94.1 2.0 copy-start.1
  96.2 0.7 copy-start.27
  96.2 0.7 copy-start.28
  96.9 16.4 %copy-start.32 = (u32[32]{0:T(128)S(1)}, u32[32]{0:T(128)}, u32[]{:S(2)}) copy-start(u32[32]{0:T(128)} %constant.139) | copy-start | bytes 388
  96.9 63.9 %copy-start.4 = (bf16[1,1,107520]{2,1,0:T(2,128)(2,1)S(1)}, bf16[1,1,107520]{2,1,0:T(2,128)(2,1)}, u32[]{:S(2)}) copy-start(bf16[1,1,107520]{2,1,0:T(2,128)(2,1)} %param.16) | copy-start | bytes 645124
  112.3 0.9 copy-start.5
  112.3 51.8 %copy-start.24 = (bf16[107520]{0:T(1024)(128)(2,1)S(1)}, bf16[107520]{0:T(1024)(128)(2,1)}, u32[]{:S(2)}) copy-start(bf16[107520]{0:T(1024)(128)(2,1)} %copy-done.23) | copy-start | bytes 645124
  112.3 55.4 %copy-start.9 = (bf16[1,3,107520]{2,1,0:T(4,128)(2,1)S(1)}, bf16[1,3,107520]{2,1,0:T(4,128)(2,1)}, u32[]{:S(2)}) copy-start(bf16[1,3,107520]{2,1,0:T(4,128)(2,1)} %param.17) | copy-start | bytes 1935364
  113.2 176.3 %all-reduce.11.cloned.1.call-start = ((), (), s32[]{:S(2)}) async-start(), calls=%async_computation.1 | async-start | bytes 1720320
  164.1 9.6 %collective-permute-start.1 = (bf16[107520]{0:T(1024)(128)(2,1)S(1)}, bf16[107520]{0:T(1024)(128)(2,1)S(1)}, u32[]{:S(2)}, u32[]{:S(2)}) collective-permute-start(bf16[107520]{0:T(1024)(128)(2,1)S(1)} %add_convert_fusion.3), channel_id=1, source_target_pairs={{0,4},{4,8},{8,12},{1,5},{5,9},{9,13},{2,6},{6,10},{10,14},{3,7},{... | collective-permute-start | bytes 645128 | tf_op jit(solution)/shard_map/ppermute | solution.py:16
  173.7 17.7 %copy-start.12 = (bf16[107520]{0:T(1024)(128)(2,1)}, bf16[107520]{0:T(1024)(128)(2,1)S(1)}, u32[]{:S(2)}) copy-start(bf16[107520]{0:T(1024)(128)(2,1)S(1)} %broadcast_select_fusion.2) | copy-start | bytes 645124
  173.7 17.7 %collective-permute-start.2 = (bf16[107520]{0:T(1024)(128)(2,1)S(1)}, bf16[107520]{0:T(1024)(128)(2,1)S(1)}, u32[]{:S(2)}, u32[]{:S(2)}) collective-permute-start(bf16[107520]{0:T(1024)(128)(2,1)S(1)} %broadcast_select_fusion.2), channel_id=1, source_target_pairs={{0,16},{16,0},{1,17},{17,1},{2,18},{18,2},{3,19},{19,3},{4,20},{20... | collective-permute-start | bytes 645128 | tf_op jit(solution)/shard_map/ppermute | solution.py:10
  223.7 2.0 copy-start.2
  225.8 0.7 copy-start.29
  242.0 0.9 copy-start.6
  242.0 49.7 %copy-start.13 = (bf16[107520]{0:T(1024)(128)(2,1)S(1)}, bf16[107520]{0:T(1024)(128)(2,1)}, u32[]{:S(2)}) copy-start(bf16[107520]{0:T(1024)(128)(2,1)} %copy-done.12) | copy-start | bytes 645124
  242.0 59.4 %copy-start.18 = (bf16[107520]{0:T(1024)(128)(2,1)S(1)}, bf16[107520]{0:T(1024)(128)(2,1)}, u32[]{:S(2)}) copy-start(bf16[107520]{0:T(1024)(128)(2,1)} %get-tuple-element.323) | copy-start | bytes 645124
  242.9 174.4 %all-reduce.13.cloned.1.call-start = ((), (), s32[]{:S(2)}) async-start(), calls=%async_computation.2 | async-start | bytes 1720320
  291.8 49.4 %copy-start.19 = (bf16[107520]{0:T(1024)(128)(2,1)}, bf16[107520]{0:T(1024)(128)(2,1)S(1)}, u32[]{:S(2)}) copy-start(bf16[107520]{0:T(1024)(128)(2,1)S(1)} %add_convert_fusion.2) | copy-start | bytes 645124
  291.8 9.6 %collective-permute-start.3 = (bf16[107520]{0:T(1024)(128)(2,1)S(1)}, bf16[107520]{0:T(1024)(128)(2,1)S(1)}, u32[]{:S(2)}, u32[]{:S(2)}) collective-permute-start(bf16[107520]{0:T(1024)(128)(2,1)S(1)} %add_convert_fusion.2), channel_id=1, source_target_pairs={{0,4},{4,8},{8,12},{1,5},{5,9},{9,13},{2,6},{6,10},{10,14},{3,7},{... | collective-permute-start | bytes 645128 | tf_op jit(solution)/shard_map/ppermute | solution.py:16
  301.4 17.7 %copy-start.14 = (bf16[107520]{0:T(1024)(128)(2,1)}, bf16[107520]{0:T(1024)(128)(2,1)S(1)}, u32[]{:S(2)}) copy-start(bf16[107520]{0:T(1024)(128)(2,1)S(1)} %broadcast_select_fusion.1) | copy-start | bytes 645124
  301.4 17.7 %collective-permute-start.4 = (bf16[107520]{0:T(1024)(128)(2,1)S(1)}, bf16[107520]{0:T(1024)(128)(2,1)S(1)}, u32[]{:S(2)}, u32[]{:S(2)}) collective-permute-start(bf16[107520]{0:T(1024)(128)(2,1)S(1)} %broadcast_select_fusion.1), channel_id=1, source_target_pairs={{0,16},{16,0},{1,17},{17,1},{2,18},{18,2},{3,19},{19,3},{4,20},{20... | collective-permute-start | bytes 645128 | tf_op jit(solution)/shard_map/ppermute | solution.py:10
  351.6 2.0 copy-start.3
  353.6 0.7 copy-start.30
  369.8 0.9 copy-start.7
  369.8 49.7 %copy-start.15 = (bf16[107520]{0:T(1024)(128)(2,1)S(1)}, bf16[107520]{0:T(1024)(128)(2,1)}, u32[]{:S(2)}) copy-start(bf16[107520]{0:T(1024)(128)(2,1)} %copy-done.14) | copy-start | bytes 645124
  369.8 59.4 %copy-start.17 = (bf16[107520]{0:T(1024)(128)(2,1)S(1)}, bf16[107520]{0:T(1024)(128)(2,1)}, u32[]{:S(2)}) copy-start(bf16[107520]{0:T(1024)(128)(2,1)} %get-tuple-element.322) | copy-start | bytes 645124
  370.7 174.3 %all-reduce.15.cloned.1.call-start = ((), (), s32[]{:S(2)}) async-start(), calls=%async_computation.3 | async-start | bytes 1720320
  419.6 49.2 %copy-start.21 = (bf16[107520]{0:T(1024)(128)(2,1)}, bf16[107520]{0:T(1024)(128)(2,1)S(1)}, u32[]{:S(2)}) copy-start(bf16[107520]{0:T(1024)(128)(2,1)S(1)} %add_convert_fusion.1) | copy-start | bytes 645124
  419.6 9.6 %collective-permute-start.5 = (bf16[107520]{0:T(1024)(128)(2,1)S(1)}, bf16[107520]{0:T(1024)(128)(2,1)S(1)}, u32[]{:S(2)}, u32[]{:S(2)}) collective-permute-start(bf16[107520]{0:T(1024)(128)(2,1)S(1)} %add_convert_fusion.1), channel_id=1, source_target_pairs={{0,4},{4,8},{8,12},{1,5},{5,9},{9,13},{2,6},{6,10},{10,14},{3,7},{... | collective-permute-start | bytes 645128 | tf_op jit(solution)/shard_map/ppermute | solution.py:16
  429.2 17.7 %copy-start.10 = (bf16[107520]{0:T(1024)(128)(2,1)}, bf16[107520]{0:T(1024)(128)(2,1)S(1)}, u32[]{:S(2)}) copy-start(bf16[107520]{0:T(1024)(128)(2,1)S(1)} %broadcast_select_fusion) | copy-start | bytes 645124
  429.2 17.7 %collective-permute-start.6 = (bf16[107520]{0:T(1024)(128)(2,1)S(1)}, bf16[107520]{0:T(1024)(128)(2,1)S(1)}, u32[]{:S(2)}, u32[]{:S(2)}) collective-permute-start(bf16[107520]{0:T(1024)(128)(2,1)S(1)} %broadcast_select_fusion), channel_id=1, source_target_pairs={{0,16},{16,0},{1,17},{17,1},{2,18},{18,2},{3,19},{19,3},{4,20},{20... | collective-permute-start | bytes 645128 | tf_op jit(solution)/shard_map/ppermute | solution.py:10
  479.2 2.0 copy-start
  481.3 0.7 copy-start.31
  481.9 16.5 %copy-start.20 = (bf16[107520]{0:T(1024)(128)(2,1)S(1)}, bf16[107520]{0:T(1024)(128)(2,1)}, u32[]{:S(2)}) copy-start(bf16[107520]{0:T(1024)(128)(2,1)} %copy-done.19) | copy-start | bytes 645124
  481.9 16.7 %copy-start.22 = (bf16[107520]{0:T(1024)(128)(2,1)S(1)}, bf16[107520]{0:T(1024)(128)(2,1)}, u32[]{:S(2)}) copy-start(bf16[107520]{0:T(1024)(128)(2,1)} %copy-done.21) | copy-start | bytes 645124
  497.5 0.9 copy-start.8
  497.5 49.7 %copy-start.11 = (bf16[107520]{0:T(1024)(128)(2,1)S(1)}, bf16[107520]{0:T(1024)(128)(2,1)}, u32[]{:S(2)}) copy-start(bf16[107520]{0:T(1024)(128)(2,1)} %copy-done.10) | copy-start | bytes 645124
  498.4 49.1 %copy-start.16 = (bf16[1,107520]{1,0:T(2,128)(2,1)S(1)}, bf16[1,107520]{1,0:T(2,128)(2,1)}, u32[]{:S(2)}) copy-start(bf16[1,107520]{1,0:T(2,128)(2,1)} %get-tuple-element.324) | copy-start | bytes 645124
Sparse Core Ops, SparseCore 0:
  113.3 47.3 all-reduce.8
  243.1 46.4 all-reduce.10
  370.9 46.4 all-reduce.12
  498.5 46.4 all-reduce.14
where the time goes:
time: 569 us; the launch traced here: 557 us
  waiting for transfers between devices  200 us (35%)
  blocking collectives  161 us (28%)
  local copies, waits for them, and re-layouts  68.4 us (12%)
  other arithmetic  60.2 us (11%)
  matrix products  40.9 us (7%)
  between operations  14.3 us (3%)
  starting transfers between devices  10.8 us (2%)
    unnamed x8, waiting for transfers between devices  186 us
    all_gather x4, blocking collectives, on_device(): own_all = lax.all_gather(own_block, 'tp', axis=0, tiled=True)  85.7 us
    all_gather x4, blocking collectives, on_device(): partner_all = lax.all_gather(partner, 'tp', axis=0, tiled=True)  75.7 us
    convert_element_type x16, local copies, waits for them, and re-layouts, normed(): values = stream.astype(jnp.float32)  23.9 us
    all_gather x1, other arithmetic, on_device(): own_all = lax.all_gather(own_block, 'tp', axis=0, tiled=True)  18.7 us
    ppermute x3, waiting for transfers between devices, shifted(): lax.ppermute(value, axis, [(source, source + steps) for source in range(i...  14.2 us
    dot_general x4, matrix products, attend(): jnp.dot(key_src, value_w, preferred_element_type=jnp.float32)  13.7 us
    dot_general x4, matrix products, attend(): jnp.dot(key_src, key_w, preferred_element_type=jnp.float32)  13.7 us
  transfers between devices with their start and end apart: 11, of which 7 were waited for; matrix products, arithmetic and copies ran while one was open for 4% of the time, Pallas kernels for 0%

commit v1 on v0

v1 whole, which is shorter than its diff:
```python
import functools

import jax
import jax.numpy as jnp
from jax import lax
from jax.experimental import pallas as pl
from jax.experimental.pallas import tpu as pltpu
from jax.sharding import PartitionSpec as P

HDIM = 64
MESH = pl.DeviceIdType.MESH
F32 = jnp.float32
BF16 = jnp.bfloat16


def remote(src, dst, send_sem, recv_sem, where):
    return pltpu.make_async_remote_copy(
        src_ref=src, dst_ref=dst, send_sem=send_sem, recv_sem=recv_sem,
        device_id=where, device_id_type=MESH,
    )


def dot_nt(a, b):
    return lax.dot_general(a, b, (((1,), (1,)), ((), ())), preferred_element_type=F32)


def attend(q_ref, k_ref, v_ref, att_ref, live):
    rows_q, joint = q_ref.shape
    rows_k = k_ref.shape[0]
    alive = lax.broadcasted_iota(jnp.int32, (rows_q, rows_k), 1) < live
    lane = lax.broadcasted_iota(jnp.int32, (1, 128), 1) // HDIM
    for at in range(0, joint, 128):
        query = q_ref[:, at:at + 128]
        keys = k_ref[:, at:at + 128]
        values = v_ref[:, at:at + 128]
        total = None
        for head in range(128 // HDIM):
            mask = (lane == head).astype(F32).astype(BF16)
            scores = dot_nt(query, keys * mask) * (HDIM ** -0.5)
            weights = jnp.exp(jnp.where(alive, scores, -1e30))
            probs = (weights / jnp.sum(weights, axis=-1, keepdims=True)).astype(BF16)
            part = jnp.dot(probs, values * mask, preferred_element_type=F32)
            total = part if total is None else total + part
        att_ref[:, at:at + 128] = total.astype(BF16)


def kernel(sections, groups, ticks, txt_len, vis_len, gain_v, gain_t, in_v, in_t, wide_hbm, narrow_hbm,
           out_v, out_t,
           wide, narrow, all_v, all_t, send_v, send_t, got_v, got_t,
           acc_v, acc_ka, acc_kb, acc_t, acc_kc, acc_kd, ssq_v, ssq_t,
           q_v, k_v, v_v, q_t, k_t, v_t,
           weight_sem, load_sem, ag_send, ag_recv, fw_send, fw_recv, rs_send, rs_recv, sh_send, sh_recv):
    tower = lax.axis_index("tower")
    section = lax.axis_index("section")
    me = lax.axis_index("tp")

    weight_copies = [
        pltpu.make_async_copy(narrow_hbm, narrow, weight_sem.at[0]),
        pltpu.make_async_copy(wide_hbm, wide, weight_sem.at[1]),
    ]

    barrier = pltpu.get_barrier_semaphore()

    def greet(d, _):
        pl.semaphore_signal(barrier, inc=1, device_id={"tp": lax.rem(me + d, groups)}, device_id_type=MESH)
        return 0

    lax.fori_loop(1, groups, greet, 0)
    pl.semaphore_signal(barrier, inc=1, device_id={"tower": 1 - tower}, device_id_type=MESH)

    @pl.when(section > 0)
    def _():
        pl.semaphore_signal(barrier, inc=1, device_id={"section": section - 1}, device_id_type=MESH)

    @pl.when(section < sections - 1)
    def _():
        pl.semaphore_signal(barrier, inc=1, device_id={"section": section + 1}, device_id_type=MESH)

    def side(vision):
        mine, other = (all_v, all_t) if vision else (all_t, all_v)
        inputs = in_v if vision else in_t
        send, got, out = (send_v, got_v, out_v) if vision else (send_t, got_t, out_t)
        gain_mine, gain_other = (gain_v, gain_t) if vision else (gain_t, gain_v)
        w_mine, w_other = (narrow, wide) if vision else (wide, narrow)
        query_w = (w_mine, 0)
        key_w, value_w = (w_other, 0), (w_other, 1)
        out_w = (w_mine, 1)
        acc_q, acc_k, acc_val = (acc_v, acc_ka, acc_kb) if vision else (acc_t, acc_kc, acc_kd)
        ssq_q, ssq_k = (ssq_v, ssq_t) if vision else (ssq_t, ssq_v)
        q_ref, k_ref, v_ref = (q_v, k_v, v_v) if vision else (q_t, k_t, v_t)
        lengths = txt_len if vision else vis_len
        part = mine.shape[-1]
        part_other = other.shape[-1]
        width = part * groups
        width_other = part_other * groups
        partner = {"tower": 1 - tower}

        def load(t):
            return pltpu.make_async_copy(inputs.at[t], mine.at[t, me], load_sem.at[t])

        load(0).start()

        @pl.when(section == 0)
        def _():
            for t in range(1, ticks):
                load(t).start()

        for copy in weight_copies:
            copy.start()

        pl.semaphore_wait(
            barrier,
            groups + (section > 0).astype(jnp.int32) + (section < sections - 1).astype(jnp.int32),
        )
        load(0).wait()

        def tick_body(t, _):
            @pl.when(t > 0)
            def _():
                @pl.when(section == 0)
                def _():
                    load(t).wait()

                @pl.when(section > 0)
                def _():
                    remote(out.at[t - 1], mine.at[t, me], sh_send.at[t - 1], sh_recv.at[t], {"section": section - 1}).wait_recv()

            def ag(d):
                return remote(mine.at[t, me], mine.at[t, me], ag_send.at[d], ag_recv.at[t, d], {"tp": lax.rem(me + d, groups)})

            def ag_in(d):
                source = lax.rem(me - d + groups, groups)
                return remote(mine.at[t, source], mine.at[t, source], ag_send.at[d], ag_recv.at[t, d], {"tp": lax.rem(me + d, groups)})

            def fw(d):
                source = lax.rem(me - d + groups, groups)
                return remote(mine.at[t, source], mine.at[t, source], fw_send.at[d], fw_recv.at[t, d], partner)

            def fw_in(d):
                source = lax.rem(me - d + groups, groups)
                return remote(other.at[t, source], other.at[t, source], fw_send.at[d], fw_recv.at[t, d], partner)

            def rs(d):
                return remote(send.at[d], got.at[t, d], rs_send.at[d], rs_recv.at[t, d], {"tp": lax.rem(me + d, groups)})

            def each(body, first=0):
                def step(d, _):
                    body(d)
                    return 0
                lax.fori_loop(first, groups, step, 0)

            each(lambda d: ag(d).start(), 1)
            fw(0).start()

            @pl.when(t == 0)
            def _():
                for copy in weight_copies:
                    copy.wait()

            acc_q[...] = jnp.zeros_like(acc_q)
            acc_k[...] = jnp.zeros_like(acc_k)
            acc_val[...] = jnp.zeros_like(acc_val)
            ssq_q[...] = jnp.zeros_like(ssq_q)
            ssq_k[...] = jnp.zeros_like(ssq_k)

            def weight_rows(w, source, count):
                ref, which = w
                return ref[which, pl.ds(pl.multiple_of(source * count, 16), count), :]

            def query_block(d):
                source = lax.rem(me - d + groups, groups)
                x = mine[t, source].astype(F32)
                ssq_q[...] += jnp.sum(x * x, axis=-1, keepdims=True)
                x = (x * gain_mine[source].astype(F32)).astype(BF16)
                acc_q[...] += jnp.dot(x, weight_rows(query_w, source, part), preferred_element_type=F32)

            def key_block(d):
                source = lax.rem(me - d + groups, groups)
                fw_in(d).wait_recv()
                x = other[t, source].astype(F32)
                ssq_k[...] += jnp.sum(x * x, axis=-1, keepdims=True)
                x = (x * gain_other[source].astype(F32)).astype(BF16)
                acc_k[...] += jnp.dot(x, weight_rows(key_w, source, part_other), preferred_element_type=F32)
                acc_val[...] += jnp.dot(x, weight_rows(value_w, source, part_other), preferred_element_type=F32)

            query_block(0)
            key_block(0)

            def arrive(d):
                ag_in(d).wait_recv()
                fw(d).start()
                query_block(d)
                key_block(d)

            each(arrive, 1)

            scale_q = lax.rsqrt(ssq_q[...] * (1.0 / width) + 1e-06)
            scale_k = lax.rsqrt(ssq_k[...] * (1.0 / width_other) + 1e-06)
            q_ref[...] = (acc_q[...] * scale_q).astype(BF16)
            k_ref[...] = (acc_k[...] * scale_k).astype(BF16)
            v_ref[...] = (acc_val[...] * scale_k).astype(BF16)
            live = lengths[t - section + sections - 1]
            attend(q_ref, k_ref, v_ref, q_ref, live)

            def project(target):
                return dot_nt(q_ref[...], weight_rows(out_w, target, part)).astype(BF16)

            def emit(d):
                send[d] = project(lax.rem(me + d, groups))
                rs(d).start()

            each(emit, 1)
            send[0] = project(me)

            def collect(d):
                rs(d).wait_recv()

            each(collect, 1)
            total = mine[t, me].astype(F32) + send[0].astype(F32)
            for d in range(1, groups):
                total = total + got[t, d].astype(F32)
            out[t] = total.astype(BF16)

            @pl.when((section < sections - 1) & (t < ticks - 1))
            def _():
                remote(out.at[t], mine.at[t + 1, me], sh_send.at[t], sh_recv.at[t + 1], {"section": section + 1}).start()

            def drain(d):
                ag(d).wait_send()
                rs(d).wait_send()
                fw(d).wait_send()

            each(drain, 1)
            fw(0).wait_send()
            return 0

        lax.fori_loop(0, ticks, tick_body, 0)

        @pl.when(section < sections - 1)
        def _():
            for t in range(ticks - 1):
                remote(out.at[t], mine.at[t + 1, me], sh_send.at[t], sh_recv.at[t + 1], {"section": section + 1}).wait_send()

    pl.when(tower == 0)(lambda: side(True))
    pl.when(tower == 1)(lambda: side(False))


def on_device(in_flight, fresh, wide_proj, narrow_proj, gain_vis, gain_txt, text_len, vis_len):
    sections = lax.axis_size("section")
    groups = lax.axis_size("tp")
    flat = in_flight.shape[2]
    ticks = fresh.shape[1] + 1
    vis_width = gain_vis.shape[1]
    txt_width = gain_txt.shape[1]
    vis_rows = flat * groups // vis_width
    txt_rows = flat * groups // txt_width
    pad_v = -(-vis_rows // 16) * 16
    pad_t = -(-txt_rows // 16) * 16
    part_v = vis_width // groups
    part_t = txt_width // groups
    joint = wide_proj.shape[-1]
    first_vis = lax.axis_index("tower") == 0

    streams = jnp.concatenate([in_flight[0, :1], fresh[0]], axis=0)
    in_v = jnp.pad(streams.reshape(ticks, vis_rows, part_v), ((0, 0), (0, pad_v - vis_rows), (0, 0)))
    in_t = jnp.pad(streams.reshape(ticks, txt_rows, part_t), ((0, 0), (0, pad_t - txt_rows), (0, 0)))
    gain_v = gain_vis[0].reshape(groups, 1, part_v)
    gain_t = gain_txt[0].reshape(groups, 1, part_t)

    vmem = pl.BlockSpec(memory_space=pltpu.VMEM)
    smem = pl.BlockSpec(memory_space=pltpu.SMEM)
    anywhere = pl.BlockSpec(memory_space=pl.ANY)
    out_v, out_t = pl.pallas_call(
        functools.partial(kernel, sections, groups, ticks),
        out_shape=(
            jax.ShapeDtypeStruct((ticks, pad_v, part_v), BF16),
            jax.ShapeDtypeStruct((ticks, pad_t, part_t), BF16),
        ),
        in_specs=[smem, smem, vmem, vmem, anywhere, anywhere, anywhere, anywhere],
        out_specs=(vmem, vmem),
        scratch_shapes=[
            pltpu.VMEM(wide_proj.shape[2:], BF16),
            pltpu.VMEM(narrow_proj.shape[2:], BF16),
            pltpu.VMEM((ticks, groups, pad_v, part_v), BF16),
            pltpu.VMEM((ticks, groups, pad_t, part_t), BF16),
            pltpu.VMEM((groups, pad_v, part_v), BF16),
            pltpu.VMEM((groups, pad_t, part_t), BF16),
            pltpu.VMEM((ticks, groups, pad_v, part_v), BF16),
            pltpu.VMEM((ticks, groups, pad_t, part_t), BF16),
            pltpu.VMEM((pad_v, joint), F32),
            pltpu.VMEM((pad_t, joint), F32),
            pltpu.VMEM((pad_t, joint), F32),
            pltpu.VMEM((pad_t, joint), F32),
            pltpu.VMEM((pad_v, joint), F32),
            pltpu.VMEM((pad_v, joint), F32),
            pltpu.VMEM((pad_v, 1), F32),
            pltpu.VMEM((pad_t, 1), F32),
            pltpu.VMEM((pad_v, joint), BF16),
            pltpu.VMEM((pad_t, joint), BF16),
            pltpu.VMEM((pad_t, joint), BF16),
            pltpu.VMEM((pad_t, joint), BF16),
            pltpu.VMEM((pad_v, joint), BF16),
            pltpu.VMEM((pad_v, joint), BF16),
            pltpu.SemaphoreType.DMA((2,)),
            pltpu.SemaphoreType.DMA((ticks,)),
            pltpu.SemaphoreType.DMA((groups,)),
            pltpu.SemaphoreType.DMA((ticks, groups)),
            pltpu.SemaphoreType.DMA((groups,)),
            pltpu.SemaphoreType.DMA((ticks, groups)),
            pltpu.SemaphoreType.DMA((groups,)),
            pltpu.SemaphoreType.DMA((ticks, groups)),
            pltpu.SemaphoreType.DMA((ticks,)),
            pltpu.SemaphoreType.DMA((ticks,)),
        ],
        compiler_params=pltpu.CompilerParams(
            collective_id=0, has_side_effects=True, vmem_limit_bytes=58 * 1024 * 1024,
        ),
    )(text_len, vis_len, gain_v, gain_t, in_v, in_t, wide_proj[0, 0], narrow_proj[0, 0])

    def as_vision():
        return out_v[:, :vis_rows].reshape(ticks, flat)

    def as_text():
        return out_t[:, :txt_rows].reshape(ticks, flat)

    return lax.cond(first_vis, as_vision, as_text).reshape(1, 1, ticks, flat)


def solution(mesh):
    placed = (
        P("tower", "section", "tp"),
        P("tower", None, "tp"),
        P("tower", "section", None, None, "tp"),
        P("tower", "section", None, None, "tp"),
        P("section", None),
        P("section", None),
        P(),
        P(),
    )
    return jax.shard_map(
        on_device,
        mesh=mesh,
        in_specs=placed,
        out_specs=P("tower", "section", None, "tp"),
        check_vma=False,
    )
```

time: 569 us -> 224 us (0.39)
  the two profiles are of different devices: /device:TPU:12 before, /device:TPU:15 now
where the time goes in v1:
time: 224 us
  Pallas kernels  214 us (96%)
  local copies, waits for them, and re-layouts  5.4 us (2%)
  other arithmetic  4.34 us (2%)
    pallas_call x1, Pallas kernels, on_device(): pl.pallas_call(functools.partial(kernel, sections, groups, ticks), out_sh...  214 us

profile of v1, /device:TPU:15, one launch (start us, length us, event | category | flops | bytes accessed | tf_op | source)
XLA Modules:
  0.0 224.1 jit_solution(8909799582637180198)
XLA Ops:
  0.0 2.2 reduce.1
  2.2 0.2 concatenate.15
  2.4 0.0 copy-start
  2.4 2.1 concatenate.16
  4.5 1.1 pad_maximum_fusion.in_v
  5.6 0.0 copy-start.2
  5.6 0.3 concatenate.18
  5.8 0.0 copy-done
  5.9 0.7 concatenate.19
  6.6 1.1 fusion.2.in_t
  7.7 0.0 copy-done.2
  7.7 0.7 reshape_squeeze.8.gain_v
  8.4 214.3 %shard_map.84 = (bf16[4,240,448]{2,1,0:T(8,128)(2,1)S(1)}, bf16[4,96,1280]{2,1,0:T(8,128)(2,1)S(1)}) custom-call(s32[7]{0:T(128)} %txt_len.1, s32[7]{0:T(128)} %vis_len.1, bf16[4,1,448]{2,1,0:T(2,128)(2,1)} %reshape_squeeze.8.gain_v, bf16[4,1,1280]{2,1,0:T(2,128)(2,1)} %bitcast.5, bf16[4,240,448]{2,1,0:T(8,128)(2,1)} %pad_maximum_fusion.in_v, ...), custom_call_target="tpu_custom_call" | custom-call | tf_op jit(solution)/shard_map/pallas_call | solution.py:273
  222.7 0.5 conditional.1
  222.7 0.1 slice.2
  222.8 0.4 reshape.19
  223.2 0.0 copy-start.1
  223.3 0.9 copy-done.1
  (1 shorter events, 0.0 us)
Async XLA Ops:
  2.4 3.4 %copy-start = (bf16[1,3,107520]{2,1,0:T(4,128)(2,1)S(1)}, bf16[1,3,107520]{2,1,0:T(4,128)(2,1)}, u32[]{:S(2)}) copy-start(bf16[1,3,107520]{2,1,0:T(4,128)(2,1)} %param.11) | copy-start | bytes 1935364
  5.6 2.1 copy-start.2
  223.2 0.9 copy-start.1

commit v2 on v1

--- a/solution.py
+++ b/solution.py
@@ -44,11 +44,11 @@
         att_ref[:, at:at + 128] = total.astype(BF16)
 
 
-def kernel(sections, groups, ticks, txt_len, vis_len, gain_v, gain_t, in_v, in_t, wide_hbm, narrow_hbm,
+def kernel(sections, groups, ticks, chunks, txt_len, vis_len, gain_v, gain_t, in_v, in_t, wide_hbm, narrow_hbm,
            out_v, out_t,
            wide, narrow, all_v, all_t, send_v, send_t, got_v, got_t,
            acc_v, acc_ka, acc_kb, acc_t, acc_kc, acc_kd, ssq_v, ssq_t,
-           q_v, k_v, v_v, q_t, k_t, v_t,
+           q_v, k_v, v_v, q_t, k_t, v_t, sum_v, sum_t,
            weight_sem, load_sem, ag_send, ag_recv, fw_send, fw_recv, rs_send, rs_recv, sh_send, sh_recv):
     tower = lax.axis_index("tower")
     section = lax.axis_index("section")
@@ -60,21 +60,15 @@
     ]
 
     barrier = pltpu.get_barrier_semaphore()
-
-    def greet(d, _):
-        pl.semaphore_signal(barrier, inc=1, device_id={"tp": lax.rem(me + d, groups)}, device_id_type=MESH)
-        return 0
-
-    lax.fori_loop(1, groups, greet, 0)
     pl.semaphore_signal(barrier, inc=1, device_id={"tower": 1 - tower}, device_id_type=MESH)
-
-    @pl.when(section > 0)
-    def _():
-        pl.semaphore_signal(barrier, inc=1, device_id={"section": section - 1}, device_id_type=MESH)
-
-    @pl.when(section < sections - 1)
-    def _():
-        pl.semaphore_signal(barrier, inc=1, device_id={"section": section + 1}, device_id_type=MESH)
+    neighbours = (me > 0, me < groups - 1, section > 0, section < sections - 1)
+    count = 1
+    for there, where in zip(neighbours, ({"tp": me - 1}, {"tp": me + 1}, {"section": section - 1}, {"section": section + 1})):
+        count = count + there.astype(jnp.int32)
+
+        @pl.when(there)
+        def _(where=where):
+            pl.semaphore_signal(barrier, inc=1, device_id=where, device_id_type=MESH)
 
     def side(vision):
         mine, other = (all_v, all_t) if vision else (all_t, all_v)
@@ -89,6 +83,7 @@
         ssq_q, ssq_k = (ssq_v, ssq_t) if vision else (ssq_t, ssq_v)
         q_ref, k_ref, v_ref = (q_v, k_v, v_v) if vision else (q_t, k_t, v_t)
         lengths = txt_len if vision else vis_len
+        acc_out = sum_v if vision else sum_t
         part = mine.shape[-1]
         part_other = other.shape[-1]
         width = part * groups
@@ -108,49 +103,65 @@
         for copy in weight_copies:
             copy.start()
 
-        pl.semaphore_wait(
-            barrier,
-            groups + (section > 0).astype(jnp.int32) + (section < sections - 1).astype(jnp.int32),
-        )
+        pl.semaphore_wait(barrier, count)
         load(0).wait()
 
+        rows = mine.shape[2] // chunks
+        last = groups - 1
+        position = (me, last - me)
+        ahead = (me + 1, me - 1)
+        behind = (me - 1, me + 1)
+
+        def piece(c):
+            return pl.ds(c * rows, rows)
+
+        def shift(t, c, where):
+            return remote(out.at[t, piece(c)], mine.at[t + 1, me, piece(c)], sh_send.at[t, c], sh_recv.at[t + 1, c], {"section": where})
+
         def tick_body(t, _):
-            @pl.when(t > 0)
+            def gather(r, k, c, source, where):
+                ref = mine.at[t, source, piece(c)]
+                return remote(ref, ref, ag_send.at[r, k, c], ag_recv.at[t, r, k, c], {"tp": where})
+
+            def gather_out(r, k, c):
+                return gather(r, k, c, (me - k, me + k)[r], ahead[r])
+
+            def gather_in(r, k, c):
+                return gather(r, k - 1, c, (me - k, me + k)[r], behind[r])
+
+            def cross(ref, source):
+                return remote(ref.at[t, source], ref.at[t, source], fw_send.at[source], fw_recv.at[t, source], partner)
+
+            def destination(r, k):
+                return (last - k + me, k - last + me)[r]
+
+            def reduce_out(r, k, c):
+                target = destination(r, k)
+                slot = target if r == 0 else jnp.where(target == me - 1, groups, target)
+                return remote(send.at[target, piece(c)], got.at[t, slot, piece(c)], rs_send.at[r, k, c], rs_recv.at[t, r, k + 1, c], {"tp": ahead[r]})
+
+            def reduce_in(r, k, c):
+                target = destination(r, k)
+                slot = target if r == 0 else jnp.where(target == me, groups, target)
+                ref = got.at[t, slot, piece(c)]
+                return slot, remote(ref, ref, rs_send.at[r, 0, c], rs_recv.at[t, r, k, c], {"tp": behind[r]})
+
+            @pl.when((t > 0) & (section == 0))
             def _():
-                @pl.when(section == 0)
-                def _():
-                    load(t).wait()
-
-                @pl.when(section > 0)
-                def _():
-                    remote(out.at[t - 1], mine.at[t, me], sh_send.at[t - 1], sh_recv.at[t], {"section": section - 1}).wait_recv()
-
-            def ag(d):
-                return remote(mine.at[t, me], mine.at[t, me], ag_send.at[d], ag_recv.at[t, d], {"tp": lax.rem(me + d, groups)})
-
-            def ag_in(d):
-                source = lax.rem(me - d + groups, groups)
-                return remote(mine.at[t, source], mine.at[t, source], ag_send.at[d], ag_recv.at[t, d], {"tp": lax.rem(me + d, groups)})
-
-            def fw(d):
-                source = lax.rem(me - d + groups, groups)
-                return remote(mine.at[t, source], mine.at[t, source], fw_send.at[d], fw_recv.at[t, d], partner)
-
-            def fw_in(d):
-                source = lax.rem(me - d + groups, groups)
-                return remote(other.at[t, source], other.at[t, source], fw_send.at[d], fw_recv.at[t, d], partner)
-
-            def rs(d):
-                return remote(send.at[d], got.at[t, d], rs_send.at[d], rs_recv.at[t, d], {"tp": lax.rem(me + d, groups)})
-
-            def each(body, first=0):
-                def step(d, _):
-                    body(d)
-                    return 0
-                lax.fori_loop(first, groups, step, 0)
-
-            each(lambda d: ag(d).start(), 1)
-            fw(0).start()
+                load(t).wait()
+
+            for c in range(chunks):
+                @pl.when((t > 0) & (section > 0))
+                def _(c=c):
+                    ref = mine.at[t, me, piece(c)]
+                    remote(ref, ref, sh_send.at[0, c], sh_recv.at[t, c], {"section": section - 1}).wait_recv()
+
+                for r in range(2):
+                    @pl.when(position[r] < last)
+                    def _(r=r, c=c):
+                        gather_out(r, 0, c).start()
+
+            cross(mine, me).start()
 
             @pl.when(t == 0)
             def _():
@@ -167,32 +178,53 @@
                 ref, which = w
                 return ref[which, pl.ds(pl.multiple_of(source * count, 16), count), :]
 
-            def query_block(d):
-                source = lax.rem(me - d + groups, groups)
+            def query_block(source):
                 x = mine[t, source].astype(F32)
                 ssq_q[...] += jnp.sum(x * x, axis=-1, keepdims=True)
                 x = (x * gain_mine[source].astype(F32)).astype(BF16)
                 acc_q[...] += jnp.dot(x, weight_rows(query_w, source, part), preferred_element_type=F32)
 
-            def key_block(d):
-                source = lax.rem(me - d + groups, groups)
-                fw_in(d).wait_recv()
+            def key_block(source):
+                cross(other, source).wait_recv()
                 x = other[t, source].astype(F32)
                 ssq_k[...] += jnp.sum(x * x, axis=-1, keepdims=True)
                 x = (x * gain_other[source].astype(F32)).astype(BF16)
                 acc_k[...] += jnp.dot(x, weight_rows(key_w, source, part_other), preferred_element_type=F32)
                 acc_val[...] += jnp.dot(x, weight_rows(value_w, source, part_other), preferred_element_type=F32)
 
-            query_block(0)
-            key_block(0)
-
-            def arrive(d):
-                ag_in(d).wait_recv()
-                fw(d).start()
-                query_block(d)
-                key_block(d)
-
-            each(arrive, 1)
+            query_block(me)
+            key_block(me)
+
+            def hop(k, _):
+                for c in range(chunks):
+                    for r in range(2):
+                        @pl.when(position[r] >= k)
+                        def _(r=r, c=c):
+                            gather_in(r, k, c).wait_recv()
+
+                            @pl.when(position[r] < last)
+                            def _():
+                                gather_out(r, k, c).start()
+
+                for r in range(2):
+                    @pl.when(position[r] >= k)
+                    def _(r=r):
+                        cross(mine, (me - k, me + k)[r]).start()
+
+                def visit(r, _):
+                    source = jnp.where(r == 0, me - k, me + k)
+
+                    @pl.when((source >= 0) & (source < groups))
+                    def _():
+                        query_block(source)
+                        key_block(source)
+
+                    return 0
+
+                lax.fori_loop(0, 2, visit, 0)
+                return 0
+
+            lax.fori_loop(1, groups, hop, 0)
 
             scale_q = lax.rsqrt(ssq_q[...] * (1.0 / width) + 1e-06)
             scale_k = lax.rsqrt(ssq_k[...] * (1.0 / width_other) + 1e-06)
@@ -203,35 +235,66 @@
             attend(q_ref, k_ref, v_ref, q_ref, live)
 
             def project(target):
-                return dot_nt(q_ref[...], weight_rows(out_w, target, part)).astype(BF16)
-
-            def emit(d):
-                send[d] = project(lax.rem(me + d, groups))
-                rs(d).start()
-
-            each(emit, 1)
-            send[0] = project(me)
-
-            def collect(d):
-                rs(d).wait_recv()
-
-            each(collect, 1)
-            total = mine[t, me].astype(F32) + send[0].astype(F32)
-            for d in range(1, groups):
-                total = total + got[t, d].astype(F32)
-            out[t] = total.astype(BF16)
-
-            @pl.when((section < sections - 1) & (t < ticks - 1))
-            def _():
-                remote(out.at[t], mine.at[t + 1, me], sh_send.at[t], sh_recv.at[t + 1], {"section": section + 1}).start()
-
-            def drain(d):
-                ag(d).wait_send()
-                rs(d).wait_send()
-                fw(d).wait_send()
-
-            each(drain, 1)
-            fw(0).wait_send()
+                send[target] = dot_nt(q_ref[...], weight_rows(out_w, target, part)).astype(BF16)
+
+            def reduce_hop(k, _):
+                def term(r, _):
+                    @pl.when(jnp.where(r == 0, me, last - me) <= k)
+                    def _():
+                        project(jnp.where(r == 0, last - k + me, k - last + me))
+
+                    return 0
+
+                lax.fori_loop(0, 2, term, 0)
+                for c in range(chunks):
+                    for r in range(2):
+                        @pl.when(position[r] <= k)
+                        def _(r=r, c=c):
+                            @pl.when(position[r] > 0)
+                            def _():
+                                slot, copy = reduce_in(r, k, c)
+                                copy.wait_recv()
+                                target = destination(r, k)
+                                total = send[target, piece(c)].astype(F32) + got[t, slot, piece(c)].astype(F32)
+                                send[target, piece(c)] = total.astype(BF16)
+
+                            reduce_out(r, k, c).start()
+
+                return 0
+
+            lax.fori_loop(0, last, reduce_hop, 0)
+            project(me)
+            for c in range(chunks):
+                acc_out[piece(c)] = mine[t, me, piece(c)].astype(F32) + send[me, piece(c)].astype(F32)
+                for r in range(2):
+                    @pl.when(position[r] > 0)
+                    def _(r=r, c=c):
+                        slot, copy = reduce_in(r, last, c)
+                        copy.wait_recv()
+                        acc_out[piece(c)] += got[t, slot, piece(c)].astype(F32)
+
+                out[t, piece(c)] = acc_out[piece(c)].astype(BF16)
+
+                @pl.when((section < sections - 1) & (t < ticks - 1))
+                def _(c=c):
+                    shift(t, c, section + 1).start()
+
+            def drain(k, _):
+                for c in range(chunks):
+                    for r in range(2):
+                        @pl.when((position[r] >= k) & (position[r] < last))
+                        def _(r=r, c=c):
+                            gather_out(r, k, c).wait_send()
+
+                        @pl.when(position[r] <= k)
+                        def _(r=r, c=c):
+                            reduce_out(r, k, c).wait_send()
+
+                cross(mine, k).wait_send()
+                return 0
+
+            lax.fori_loop(0, last, drain, 0)
+            cross(mine, last).wait_send()
             return 0
 
         lax.fori_loop(0, ticks, tick_body, 0)
@@ -239,7 +302,8 @@
         @pl.when(section < sections - 1)
         def _():
             for t in range(ticks - 1):
-                remote(out.at[t], mine.at[t + 1, me], sh_send.at[t], sh_recv.at[t + 1], {"section": section + 1}).wait_send()
+                for c in range(chunks):
+                    shift(t, c, section + 1).wait_send()
 
     pl.when(tower == 0)(lambda: side(True))
     pl.when(tower == 1)(lambda: side(False))
@@ -259,6 +323,7 @@
     part_v = vis_width // groups
     part_t = txt_width // groups
     joint = wide_proj.shape[-1]
+    chunks = 3 if groups <= 8 and pad_v % 48 == 0 and pad_t % 48 == 0 else 1
     first_vis = lax.axis_index("tower") == 0
 
     streams = jnp.concatenate([in_flight[0, :1], fresh[0]], axis=0)
@@ -271,7 +336,7 @@
     smem = pl.BlockSpec(memory_space=pltpu.SMEM)
     anywhere = pl.BlockSpec(memory_space=pl.ANY)
     out_v, out_t = pl.pallas_call(
-        functools.partial(kernel, sections, groups, ticks),
+        functools.partial(kernel, sections, groups, ticks, chunks),
         out_shape=(
             jax.ShapeDtypeStruct((ticks, pad_v, part_v), BF16),
             jax.ShapeDtypeStruct((ticks, pad_t, part_t), BF16),
@@ -285,8 +350,8 @@
             pltpu.VMEM((ticks, groups, pad_t, part_t), BF16),
             pltpu.VMEM((groups, pad_v, part_v), BF16),
             pltpu.VMEM((groups, pad_t, part_t), BF16),
-            pltpu.VMEM((ticks, groups, pad_v, part_v), BF16),
-            pltpu.VMEM((ticks, groups, pad_t, part_t), BF16),
+            pltpu.VMEM((ticks, groups + 1, pad_v, part_v), BF16),
+            pltpu.VMEM((ticks, groups + 1, pad_t, part_t), BF16),
             pltpu.VMEM((pad_v, joint), F32),
             pltpu.VMEM((pad_t, joint), F32),
             pltpu.VMEM((pad_t, joint), F32),
@@ -301,16 +366,18 @@
             pltpu.VMEM((pad_t, joint), BF16),
             pltpu.VMEM((pad_v, joint), BF16),
             pltpu.VMEM((pad_v, joint), BF16),
+            pltpu.VMEM((pad_v, part_v), F32),
+            pltpu.VMEM((pad_t, part_t), F32),
             pltpu.SemaphoreType.DMA((2,)),
             pltpu.SemaphoreType.DMA((ticks,)),
+            pltpu.SemaphoreType.DMA((2, groups, chunks)),
+            pltpu.SemaphoreType.DMA((ticks, 2, groups, chunks)),
             pltpu.SemaphoreType.DMA((groups,)),
             pltpu.SemaphoreType.DMA((ticks, groups)),
-            pltpu.SemaphoreType.DMA((groups,)),
-            pltpu.SemaphoreType.DMA((ticks, groups)),
-            pltpu.SemaphoreType.DMA((groups,)),
-            pltpu.SemaphoreType.DMA((ticks, groups)),
-            pltpu.SemaphoreType.DMA((ticks,)),
-            pltpu.SemaphoreType.DMA((ticks,)),
+            pltpu.SemaphoreType.DMA((2, groups, chunks)),
+            pltpu.SemaphoreType.DMA((ticks, 2, groups, chunks)),
+            pltpu.SemaphoreType.DMA((ticks, chunks)),
+            pltpu.SemaphoreType.DMA((ticks, chunks)),
         ],
         compiler_params=pltpu.CompilerParams(
             collective_id=0, has_side_effects=True, vmem_limit_bytes=58 * 1024 * 1024,

time: 224 us -> 172 us (0.77)
  the two profiles are of different devices: /device:TPU:15 before, /device:TPU:12 now
where the time goes in v2:
time: 172 us
  Pallas kernels  161 us (94%)
  local copies, waits for them, and re-layouts  6.02 us (4%)
  other arithmetic  4.34 us (3%)
    pallas_call x1, Pallas kernels, on_device(): pl.pallas_call(functools.partial(kernel, sections, groups, ticks, chunks)...  161 us

profile of v2, /device:TPU:12, one launch (start us, length us, event | category | flops | bytes accessed | tf_op | source)
XLA Modules:
  0.0 171.9 jit_solution(17230415999233726382)
XLA Ops:
  0.0 2.2 %reduce.1 = bf16[107520]{0:T(1024)(128)(2,1)S(1)} reduce(bf16[1,1,107520]{2,1,0:T(2,128)(2,1)} %param.10, bf16[]{:T(256)} %constant.18), dimensions={0,1}, to_apply=%param.10.reduce_sub_computation | reduce | bytes 430082 | tf_op args[0]
  2.2 0.2 concatenate.15
  2.4 0.0 copy-start
  2.4 2.1 %concatenate.16 = bf16[3,240,448]{2,1,0:T(8,128)(2,1)S(1)} reshape(bf16[1,3,107520]{2,1,0:T(4,128)(2,1)} %param.11) | data formatting | bytes 1290240 | tf_op jit(solution)/shard_map/concatenate | solution.py:329
  4.5 1.1 pad_maximum_fusion.in_v
  5.6 0.0 copy-start.2
  5.6 0.3 concatenate.18
  5.8 0.0 copy-done
  5.9 0.7 concatenate.19
  6.6 1.1 fusion.2.in_t
  7.7 0.0 copy-done.2
  7.7 0.7 reshape_squeeze.8.gain_v
  8.4 161.5 %shard_map.84 = (bf16[4,240,448]{2,1,0:T(8,128)(2,1)S(1)}, bf16[4,96,1280]{2,1,0:T(8,128)(2,1)S(1)}) custom-call(s32[7]{0:T(128)} %txt_len.1, s32[7]{0:T(128)} %vis_len.1, bf16[4,1,448]{2,1,0:T(2,128)(2,1)} %reshape_squeeze.8.gain_v, bf16[4,1,1280]{2,1,0:T(2,128)(2,1)} %bitcast.5, bf16[4,240,448]{2,1,0:T(8,128)(2,1)} %pad_maximum_fusion.in_v, ...), custom_call_target="tpu_custom_call" | custom-call | tf_op jit(solution)/shard_map/pallas_call | solution.py:338
  169.9 1.1 conditional.1
  169.9 1.1 reshape.20
  171.0 0.0 copy-start.1
  171.0 0.9 copy-done.1
  (1 shorter events, 0.0 us)
Async XLA Ops:
  2.4 3.4 %copy-start = (bf16[1,3,107520]{2,1,0:T(4,128)(2,1)S(1)}, bf16[1,3,107520]{2,1,0:T(4,128)(2,1)}, u32[]{:S(2)}) copy-start(bf16[1,3,107520]{2,1,0:T(4,128)(2,1)} %param.11) | copy-start | bytes 1935364
  5.6 2.1 %copy-start.2 = (bf16[1,1792]{1,0:T(2,128)(2,1)S(1)}, bf16[1,1792]{1,0:T(2,128)(2,1)}, u32[]{:S(2)}) copy-start(bf16[1,1792]{1,0:T(2,128)(2,1)} %param.14) | copy-start | bytes 10756
  171.0 0.9 copy-start.1

commit v3 on v2

--- a/solution.py
+++ b/solution.py
@@ -327,8 +327,14 @@
     first_vis = lax.axis_index("tower") == 0
 
     streams = jnp.concatenate([in_flight[0, :1], fresh[0]], axis=0)
-    in_v = jnp.pad(streams.reshape(ticks, vis_rows, part_v), ((0, 0), (0, pad_v - vis_rows), (0, 0)))
-    in_t = jnp.pad(streams.reshape(ticks, txt_rows, part_t), ((0, 0), (0, pad_t - txt_rows), (0, 0)))
+    def shaped(rows, padded, part):
+        return jnp.pad(streams.reshape(ticks, rows, part), ((0, 0), (0, padded - rows), (0, 0)))
+
+    in_v, in_t = lax.cond(
+        first_vis,
+        lambda: (shaped(vis_rows, pad_v, part_v), jnp.zeros((ticks, pad_t, part_t), BF16)),
+        lambda: (jnp.zeros((ticks, pad_v, part_v), BF16), shaped(txt_rows, pad_t, part_t)),
+    )
     gain_v = gain_vis[0].reshape(groups, 1, part_v)
     gain_t = gain_txt[0].reshape(groups, 1, part_t)
 

time: 172 us -> 167 us (0.971)
  local copies, waits for them, and re-layouts: 6.02 us -> 3.84 us
  other arithmetic: 4.34 us -> 2.19 us
    concatenate x4 -> x0, local copies, waits for them, and re-layouts: 3.3 us -> none  [on_device(): streams = jnp.concatenate([in_flight[0, :1], fresh[0]], axis=0)]
    unnamed x2 -> x1, other arithmetic: 2.23 us -> 0.03 us
where the time goes in v3:
time: 167 us
  Pallas kernels  161 us (96%)
  local copies, waits for them, and re-layouts  3.84 us (2%)
  other arithmetic  2.19 us (1%)
    pallas_call x1, Pallas kernels, on_device(): pl.pallas_call(functools.partial(kernel, sections, groups, ticks, chunks)...  161 us

profile of v3, /device:TPU:12, one launch (start us, length us, event | category | flops | bytes accessed | tf_op | source)
XLA Modules:
  0.0 167.0 jit_solution(16071969228941942158)
XLA Ops:
  0.0 2.2 %pad_maximum_fusion = bf16[4,107520]{1,0:T(4,128)(2,1)S(1)} fusion(bf16[3,107520]{1,0:T(4,128)(2,1)} %bitcast.7, bf16[1,107520]{1,0:T(2,128)(2,1)} %bitcast.8), kind=kLoop, calls=%fused_computation | loop fusion | flops 1720320 | bytes 1720320 | tf_op jit(solution)/shard_map/concatenate | solution.py:329
  2.2 0.0 copy-start.1
  2.2 1.2 conditional.2
  2.2 1.1 reshape.14
  3.3 0.1 broadcast.7
  3.3 0.0 copy-done.1
  3.4 0.7 reshape_squeeze.8.gain_v
  4.1 160.9 %shard_map.84 = (bf16[4,240,448]{2,1,0:T(8,128)(2,1)S(1)}, bf16[4,96,1280]{2,1,0:T(8,128)(2,1)S(1)}) custom-call(s32[7]{0:T(128)} %txt_len.1, s32[7]{0:T(128)} %vis_len.1, bf16[4,1,448]{2,1,0:T(2,128)(2,1)} %reshape_squeeze.8.gain_v, bf16[4,1,1280]{2,1,0:T(2,128)(2,1)} %bitcast.9, bf16[4,240,448]{2,1,0:T(8,128)(2,1)S(1)} %get-tuple-element.17.in_v, ...), custom_call_target="tpu_custom_call" | custom-call | tf_op jit(solution)/shard_map/pallas_call | solution.py:344
  165.0 1.1 conditional.3
  165.0 1.1 reshape.16
  166.1 0.0 copy-start
  166.1 0.9 copy-done
  (1 shorter events, 0.0 us)
Async XLA Ops:
  2.2 1.2 copy-start.1
  166.1 0.9 copy-start
